TPU v7x, 256 devices: a whole 4x4x8 slice. The times are simulated.
256 devices in a mesh: pair: 8 (over x, core), node: 32 (over z, y).
Axes of the slice: x: 4, y: 4, z: 8, core: 2. Of those that a mesh axis runs over, the one named last changes fastest.
Arguments:
- features: bfloat16 [32768, 256], P('node', 'pair'), may hold values from -60 to 60
- neighbors: int32 [8, 32768, 10], P('pair', 'node'), may hold values from 0 to 32767, as said below
- counts: int32 [8, 32768], P('pair', 'node'), may hold values from 1 to 10
- pairs: int32 [1048576, 2], P(('pair', 'node')), may hold values from 0 to 32767, as said below
- w_self: bfloat16 [256, 256], replicated, may hold values from -0.25 to 0.25
- w_neigh: bfloat16 [256, 256], replicated, may hold values from -0.25 to 0.25
- b_layer: float32 [256], replicated, may hold values from -3 to 3
- w_one: bfloat16 [256, 256], replicated, may hold values from -0.375 to 0.375
- b_one: float32 [256], replicated, may hold values from -3 to 3
- w_two: bfloat16 [256, 256], replicated, may hold values from -0.375 to 0.375
- b_two: float32 [256], replicated, may hold values from -3 to 3
- w_out: float32 [256], replicated, may hold values from -0.375 to 0.375
Outputs:
- pair_loss: float32 [1048576], P(('pair', 'node'))
Inputs may be any that keep to these rules, and one draw needn't show every extreme that they name: `neighbors`: within one list block (one micro-batch, the 1024 nodes of one node range) at most 640 slots name nodes of any one node range; in every micro-batch one node range receives exactly 640 from every block. `pairs`: within the 4096 rows of one device at most 512 endpoints lie in any one node range; in every micro-batch one node range receives exactly 512 from every device.
All inputs are finite; a program needn't handle non-finite values.
Results may differ from a plain program's by a relative error of at most 0.0032.
Values may be sent and summed in bfloat16 or wider, within the bound.
No kernel may reach another device: no remote copies, remote signals or barrier semaphores. Data moves between devices by JAX's collectives and lax.ppermute only.
A program may use at most 128 MiB of HBM per device.

v0:
```python
import functools
import jax
import jax.numpy as jnp
from jax import lax
from jax.experimental import pallas as pl
from jax.experimental.pallas import tpu as pltpu
from jax.sharding import PartitionSpec as P

QUARTERS = 4
FAN = 10
WORDS = FAN // 2
STEP = 16
MOVES = 32
STEPS = (8, 8, 8, 8, 8, 8, 8, 8, 8, 8)
SMEM = pl.BlockSpec(memory_space=pltpu.SMEM)
VMEM = pl.BlockSpec(memory_space=pltpu.VMEM)
ANY = pl.BlockSpec(memory_space=pl.ANY)


def look_up_kernel(where, values, out, *, step):
    def body(t, carry):
        for u in range(step):
            out[t * step + u] = values[where[t * step + u]]
        return carry

    lax.fori_loop(0, where.shape[0] // step, body, 0)


def look_up(where, values):
    return pl.pallas_call(
        functools.partial(look_up_kernel, step=STEP),
        out_shape=jax.ShapeDtypeStruct(where.shape, jnp.int32),
        in_specs=[SMEM] * 2,
        out_specs=SMEM,
        cost_estimate=pl.CostEstimate(flops=0, bytes_accessed=2**25, transcendentals=0),
    )(where, values)


def score_kernel(*refs, npair):
    starts, spots, moves, ids_hbm = refs[:4]
    table, mats, vecs, out, tab, means, sums, selfs, tab_sem, ids_sem = refs[4:14]
    ids = refs[14:]
    part = ids_hbm.shape[0] // (QUARTERS * WORDS)

    def fetch(q):
        slot = q & 1
        return [
            pltpu.make_async_copy(
                ids_hbm.at[pl.ds((q * WORDS + j) * part, part)],
                ids[j].at[pl.ds(slot * part, part)],
                ids_sem.at[slot, j],
            )
            for j in range(WORDS)
        ]

    for copy in fetch(0):
        copy.start()
    pltpu.make_async_copy(table, tab, tab_sem).start()
    pltpu.make_async_copy(table, tab, tab_sem).wait()

    def load(n):
        return tab[n].astype(jnp.float32)

    def one(i, c):
        spot = spots[i]
        words = [ids[j][spot] for j in range((c + 1) // 2)]
        rows = [
            load(lax.shift_right_logical(words[j // 2], 16) if j % 2 else words[j // 2] & 65535)
            for j in range(c)
        ]
        while len(rows) > 1:
            rows = [sum(rows[k + 1 : k + 2], rows[k]) for k in range(0, len(rows), 2)]
        return rows[0] if c == 1 else rows[0] * jnp.float32(1.0 / c)

    def quarter(q, carry):
        for copy in fetch(q):
            copy.wait()

        @pl.when(q < QUARTERS - 1)
        def _():
            for copy in fetch(q + 1):
                copy.start()

        for c in range(1, FAN + 1):
            lo = starts[q * FAN + c - 1]
            hi = starts[q * FAN + c]
            step = STEPS[c - 1]

            def body(i, c=c, step=step):
                got = [one(i + u, c) for u in range(step)]
                for u in range(step):
                    means[pl.ds(2 * i + 2 * u, 2), :] = got[u]
                return i + step

            def rest(i, c=c):
                means[pl.ds(2 * i, 2), :] = one(i, c)
                return i + 1

            lo = lax.while_loop(lambda i: i <= hi - step, body, lo)
            lax.while_loop(lambda i: i < hi, rest, lo)
        return carry

    lax.fori_loop(0, QUARTERS, quarter, 0)

    def own(t, carry):
        i = t * MOVES
        move = [moves[i + u] for u in range(MOVES)]
        got = [load(move[u] & 65535) for u in range(MOVES)]
        for u in range(MOVES):
            selfs[pl.ds(2 * i + 2 * u, 2), :] = got[u]
        got = [means[pl.ds(2 * i + 2 * u, 2), :] for u in range(MOVES)]
        for u in range(MOVES):
            e2 = pl.multiple_of(lax.shift_right_logical(move[u], 16), 2)
            sums[pl.ds(e2, 2), :] = got[u]
        return carry

    lax.fori_loop(0, 2 * npair // MOVES, own, 0)

    rows = 512

    def dense(t, carry):
        embs = []
        for side in range(2):
            r0 = (side * npair + t * rows) * 2
            x = jnp.concatenate(
                [
                    ref[pl.ds(r0 + h, rows, 2), :].astype(jnp.bfloat16)
                    for ref in (selfs, sums)
                    for h in range(2)
                ],
                axis=1,
            )
            pre = jnp.dot(x, mats[:512], preferred_element_type=jnp.float32) + vecs[0:1]
            act = jnp.maximum(pre, 0.0)
            ms = jnp.mean(act * act, axis=-1, keepdims=True)
            embs.append((act * lax.rsqrt(ms + 1e-6)).astype(jnp.bfloat16).astype(jnp.float32))
        had = (embs[0] * embs[1]).astype(jnp.bfloat16)
        first = jnp.dot(had, mats[512:768], preferred_element_type=jnp.float32) + vecs[1:2]
        first = jnp.maximum(first, 0.0).astype(jnp.bfloat16)
        second = jnp.dot(first, mats[768:], preferred_element_type=jnp.float32) + vecs[2:3]
        second = jnp.maximum(second, 0.0) * vecs[3:4]
        logit = lax.dot_general(
            jnp.ones((8, 128), jnp.float32),
            second[:, :128] + second[:, 128:],
            (((1,), (1,)), ((), ())),
            precision=lax.Precision.HIGHEST,
            preferred_element_type=jnp.float32,
        )[:1]
        k = t * rows + lax.broadcasted_iota(jnp.int32, (1, rows), 1)
        x = jnp.where(k < npair // 4, -logit, logit)
        out[pl.ds(t, 1), :] = jnp.maximum(x, 0.0) + jnp.log1p(jnp.exp(-jnp.abs(x)))
        return carry

    lax.fori_loop(0, npair // rows, dense, 0)


def score(starts, spots, moves, ids, table, mats, vecs, npair):
    nodes = table.shape[0]
    return pl.pallas_call(
        functools.partial(score_kernel, npair=npair),
        out_shape=jax.ShapeDtypeStruct((npair // 512, 512), jnp.float32),
        in_specs=[SMEM] * 3 + [ANY] * 2 + [VMEM] * 2,
        out_specs=VMEM,
        scratch_shapes=[
            pltpu.VMEM((nodes, 2, 128), jnp.bfloat16),
            pltpu.VMEM((4 * npair, 128), jnp.float32),
            pltpu.VMEM((4 * npair, 128), jnp.float32),
            pltpu.VMEM((4 * npair, 128), jnp.float32),
            pltpu.SemaphoreType.DMA,
            pltpu.SemaphoreType.DMA((2, WORDS)),
        ]
        + [pltpu.SMEM((2 * ids.shape[0] // (QUARTERS * WORDS),), jnp.int32)] * WORDS,
        compiler_params=pltpu.CompilerParams(vmem_limit_bytes=56 * 2**20),
    )(starts, spots, moves, ids, table, mats, vecs)


def on_device(
    features, neighbors, counts, pairs, w_self, w_neigh, b_layer, w_one, b_one, w_two, b_two, w_out
):
    span, cols = features.shape
    parts, shards = lax.axis_size("pair"), lax.axis_size("node")
    npair = pairs.shape[0]
    slab = lax.all_to_all(
        features.reshape(parts, span // parts, cols), "pair", split_axis=0, concat_axis=0, tiled=True
    )
    slab = slab.transpose(1, 0, 2).reshape(span // parts, 2, parts * cols // 2)
    table = lax.all_gather(slab, ("node", "pair"), axis=0, tiled=True)
    ids = neighbors[0].T
    info = jnp.concatenate([ids[0::2] | (ids[1::2] << 16), counts], axis=0)
    info = lax.all_gather(info, "node", axis=0)
    share = span * shards // QUARTERS
    ids = info[:, :WORDS].reshape(QUARTERS, -1, WORDS, span).transpose(0, 2, 1, 3).reshape(-1)
    ends = pairs.T.reshape(-1)
    code = ends // share * FAN + look_up(ends, info[:, WORDS].reshape(-1)) - 1
    keys = ((code - 32) << 26) | ((ends & (share - 1)) << 13) | jnp.arange(2 * npair, dtype=jnp.int32)
    keys = lax.sort(keys)
    marks = jnp.arange(QUARTERS * FAN + 1, dtype=jnp.int32)
    starts = jnp.sum((code[None, :] < marks[:, None]).astype(jnp.int32), axis=1)
    moves = ends | ((keys & 8191) << 17)
    spots = ((keys >> 13) & (share - 1)) + (((keys >> 26) + 32) // FAN & 1) * share
    mats = jnp.concatenate([w_self, w_neigh, w_one, w_two], axis=0)
    vecs = jnp.stack([b_layer, b_one, b_two, w_out])
    loss = score(starts, spots, moves, ids, table, mats, vecs, npair)
    return loss.reshape(-1)


def solution(mesh):
    in_specs = (
        P("node", "pair"),
        P("pair", "node", None),
        P("pair", "node"),
        P(("pair", "node"), None),
    ) + (P(),) * 8
    return jax.shard_map(
        on_device, mesh=mesh, in_specs=in_specs, out_specs=P(("pair", "node")), check_vma=False
    )
```

profile of v0, /device:TPU:1, one launch (start us, length us, event | category | flops | bytes accessed | tf_op | source)
XLA Modules:
  0.0 235.0 jit_solution(1230312167174640267)
XLA Ops:
  6.5 0.8 copy-done
  7.4 10.5 %all_to_all.5 = bf16[8,128,32]{1,2,0:T(8,128)(2,1)S(1)} all-to-all(bf16[8,128,32]{1,2,0:T(8,128)(2,1)S(1)} %copy_bitcast_fusion), channel_id=1, replica_groups=mesh['pair'=8,'node'=32] {'pair'}, dimensions={0} | all-to-all | bytes 131072 | tf_op jit(solution)/shard_map/all_to_all | solution.py:183
  17.9 0.7 copy.24
  18.6 0.0 all-gather.4.cloned.1.call-update
  18.6 0.8 copy.32
  19.5 1.4 copy.27
  20.8 0.7 add_bitcast_fusion
  21.5 43.1 %all-gather.1 = s32[32,6,1024]{2,1,0:T(8,128)S(1)} all-gather(s32[1,6,1024]{2,1,0:T(8,128)S(1)} %add_bitcast_fusion), channel_id=2, replica_groups=mesh['pair'=8,'node'=32] {'node'}, dimensions={0}, use_global_device_ids=true | all-gather | bytes 811008 | tf_op jit(solution)/shard_map/all_gather | solution.py:190
  64.7 0.8 slice.16
  65.5 0.0 copy-start.9
  65.5 0.0 copy-start.4
  65.5 0.0 copy-start.5
  65.5 0.4 copy.22
  65.9 1.0 copy.28
  66.9 19.2 %shard_map.118 = s32[8192]{0:T(1024)} custom-call(s32[8192]{0:T(1024)} %bitcast.34, s32[32768]{0:T(1024)} %bitcast.33), custom_call_target="tpu_custom_call" | custom-call | bytes 33554432 | tf_op jit(solution)/shard_map/pallas_call | solution.py:30
  86.1 0.8 iota_or_fusion
  86.9 6.8 %sort.14 = (s32[8192]{0:T(1024)S(1)}, s32[8192]{0:T(1024)}) sort(s32[8192]{0:T(1024)S(1)} %get-tuple-element.8, s32[8192]{0:T(1024)S(1)} %iota.11), dimensions={0}, to_apply=%region_1.2 | sort | flops 106496 | bytes 131072 | tf_op jit(solution)/shard_map/sort | solution.py:196
  93.7 0.6 pad_maximum_fusion.1.refs_6_
  94.4 0.8 pad_maximum_fusion.refs_5_
  95.2 0.8 convert_reduce_fusion.refs_0_
  96.0 0.7 shift-left_or_fusion
  96.6 48.7 %all-gather.4.cloned.1.call-done.refs_4_ = bf16[32768,2,128]{2,1,0:T(2,128)(2,1)} async-done(((bf16[128,2,128]{2,1,0:T(2,128)(2,1)}), bf16[32768,2,128]{2,1,0:T(2,128)(2,1)}) %all-gather.4.cloned.1.call-update) | async-done | bytes 16777232 | tf_op jit(solution)/shard_map/all_gather | solution.py:187
  145.3 81.5 %shard_map.119 = f32[8,512]{1,0:T(8,128)} custom-call(s32[41]{0:T(128)} %convert_reduce_fusion.refs_0_, s32[8192]{0:T(1024)} %get-tuple-element.11.refs_1_, s32[8192]{0:T(1024)} %get-tuple-element.10.refs_2_, s32[163840]{0:T(1024)} %bitcast.31, bf16[32768,2,128]{2,1,0:T(2,128)(2,1)} %all-gather.4.cloned.1.call-done.refs_4_, ...), custom_call_target="tpu_custom_call" | custom-call | tf_op jit(solution)/shard_map/pallas_call | solution.py:159
  226.9 1.3 copy.29
  (22 shorter events, 0.1 us)
Async XLA Ops:
  6.5 0.8 copy-start
  6.5 138.8 %all-gather.4.cloned.1.call-start = ((), (), s32[]{:S(2)}) async-start(), calls=%async_computation.1 | async-start | bytes 16842752 | tf_op jit(solution)/shard_map/all_gather | solution.py:187
  65.5 20.7 %copy-start.1 = (s32[1,32,2,128]{3,1,2,0:T(8,128)S(1)}, s32[1,32,2,128]{3,1,2,0:T(8,128)}, u32[]{:S(2)}) copy-start(s32[1,32,2,128]{3,1,2,0:T(8,128)} %copy.27) | copy-start | bytes 98308
  65.5 28.3 %copy-start.6 = (f32[256]{0:T(256)S(1)}, f32[256]{0:T(256)}, u32[]{:S(2)}) copy-start(f32[256]{0:T(256)} %param.23) | copy-start | bytes 3076
  65.5 28.3 %copy-start.7 = (f32[256]{0:T(256)S(1)}, f32[256]{0:T(256)}, u32[]{:S(2)}) copy-start(f32[256]{0:T(256)} %param.22) | copy-start | bytes 3076
  65.5 28.3 %copy-start.8 = (f32[256]{0:T(256)S(1)}, f32[256]{0:T(256)}, u32[]{:S(2)}) copy-start(f32[256]{0:T(256)} %param.20) | copy-start | bytes 3076
  65.5 28.3 %copy-start.9 = (f32[256]{0:T(256)S(1)}, f32[256]{0:T(256)}, u32[]{:S(2)}) copy-start(f32[256]{0:T(256)} %param.18) | copy-start | bytes 3076
  65.5 28.9 %copy-start.2 = (bf16[256,256]{1,0:T(8,128)(2,1)S(1)}, bf16[256,256]{1,0:T(8,128)(2,1)}, u32[]{:S(2)}) copy-start(bf16[256,256]{1,0:T(8,128)(2,1)} %param.21) | copy-start | bytes 393220
  65.5 28.8 %copy-start.3 = (bf16[256,256]{1,0:T(8,128)(2,1)S(1)}, bf16[256,256]{1,0:T(8,128)(2,1)}, u32[]{:S(2)}) copy-start(bf16[256,256]{1,0:T(8,128)(2,1)} %param.19) | copy-start | bytes 393220
  65.5 28.8 %copy-start.4 = (bf16[256,256]{1,0:T(8,128)(2,1)S(1)}, bf16[256,256]{1,0:T(8,128)(2,1)}, u32[]{:S(2)}) copy-start(bf16[256,256]{1,0:T(8,128)(2,1)} %param.17) | copy-start | bytes 393220
  65.5 28.8 %copy-start.5 = (bf16[256,256]{1,0:T(8,128)(2,1)S(1)}, bf16[256,256]{1,0:T(8,128)(2,1)}, u32[]{:S(2)}) copy-start(bf16[256,256]{1,0:T(8,128)(2,1)} %param.16) | copy-start | bytes 393220
Sparse Core Ops, SparseCore 0:
  18.7 126.5 all-gather.3
where the time goes:
time: 235 us
  Pallas kernels  101 us (43%)
  blocking collectives  53.6 us (23%)
  waiting for transfers between devices  48.7 us (21%)
  between operations  13.5 us (6%)
  other arithmetic  11.2 us (5%)
  local copies, waits for them, and re-layouts  7.33 us (3%)
    pallas_call x1, Pallas kernels, score(): pl.pallas_call(functools.partial(score_kernel, npair=npair), out_shape=ja...  81.5 us
    all_gather x1, waiting for transfers between devices, on_device(): table = lax.all_gather(slab, ('node', 'pair'), axis=0, tiled=True)  48.7 us
    all_gather x1, blocking collectives, on_device(): info = lax.all_gather(info, 'node', axis=0)  43.1 us
    pallas_call x1, Pallas kernels, look_up(): pl.pallas_call(functools.partial(look_up_kernel, step=STEP), out_shape=ja...  19.2 us
    all_to_all x1, blocking collectives, on_device(): lax.all_to_all(features.reshape(parts, span // parts, cols), 'pair', spli...  10.5 us
    sort x1, other arithmetic, on_device(): keys = lax.sort(keys)  6.77 us
    unnamed x24, local copies, waits for them, and re-layouts  5.36 us
  transfers between devices with their start and end apart: 1, of which 1 were waited for; matrix products, arithmetic and copies ran while one was open for 7% of the time, Pallas kernels for 8%

commit v1 on v0

--- a/solution.py
+++ b/solution.py
@@ -11,7 +11,8 @@
 WORDS = FAN // 2
 STEP = 16
 MOVES = 32
-STEPS = (8, 8, 8, 8, 8, 8, 8, 8, 8, 8)
+ROWS = 1024
+STEPS = (12, 12, 12, 12, 12, 12, 12, 12, 12, 12)
 SMEM = pl.BlockSpec(memory_space=pltpu.SMEM)
 VMEM = pl.BlockSpec(memory_space=pltpu.VMEM)
 ANY = pl.BlockSpec(memory_space=pl.ANY)
@@ -37,9 +38,9 @@
 
 
 def score_kernel(*refs, npair):
-    starts, spots, moves, ids_hbm = refs[:4]
-    table, mats, vecs, out, tab, means, sums, selfs, tab_sem, ids_sem = refs[4:14]
-    ids = refs[14:]
+    starts, spots_hbm, moves_hbm, ids_hbm = refs[:4]
+    table, mats, vecs, out, tab, means, sums, selfs, tab_sem, ids_sem, list_sem, spots, moves = refs[4:17]
+    ids = refs[17:]
     part = ids_hbm.shape[0] // (QUARTERS * WORDS)
 
     def fetch(q):
@@ -55,8 +56,16 @@
 
     for copy in fetch(0):
         copy.start()
+    lists = [
+        pltpu.make_async_copy(spots_hbm, spots, list_sem.at[0]),
+        pltpu.make_async_copy(moves_hbm, moves, list_sem.at[1]),
+    ]
+    for copy in lists:
+        copy.start()
     pltpu.make_async_copy(table, tab, tab_sem).start()
     pltpu.make_async_copy(table, tab, tab_sem).wait()
+    for copy in lists:
+        copy.wait()
 
     def load(n):
         return tab[n].astype(jnp.float32)
@@ -105,18 +114,15 @@
     def own(t, carry):
         i = t * MOVES
         move = [moves[i + u] for u in range(MOVES)]
-        got = [load(move[u] & 65535) for u in range(MOVES)]
         for u in range(MOVES):
-            selfs[pl.ds(2 * i + 2 * u, 2), :] = got[u]
-        got = [means[pl.ds(2 * i + 2 * u, 2), :] for u in range(MOVES)]
-        for u in range(MOVES):
-            e2 = pl.multiple_of(lax.shift_right_logical(move[u], 16), 2)
-            sums[pl.ds(e2, 2), :] = got[u]
+            selfs[pl.ds(2 * i + 2 * u, 2), :] = load(move[u] & 65535)
+            mean = pl.multiple_of(lax.shift_right_logical(move[u], 16), 2)
+            sums[pl.ds(2 * i + 2 * u, 2), :] = means[pl.ds(mean, 2), :]
         return carry
 
     lax.fori_loop(0, 2 * npair // MOVES, own, 0)
 
-    rows = 512
+    rows = ROWS
 
     def dense(t, carry):
         embs = []
@@ -148,7 +154,9 @@
         )[:1]
         k = t * rows + lax.broadcasted_iota(jnp.int32, (1, rows), 1)
         x = jnp.where(k < npair // 4, -logit, logit)
-        out[pl.ds(t, 1), :] = jnp.maximum(x, 0.0) + jnp.log1p(jnp.exp(-jnp.abs(x)))
+        x = jnp.maximum(x, 0.0) + jnp.log1p(jnp.exp(-jnp.abs(x)))
+        for u in range(rows // 128):
+            out[pl.ds(t * (rows // 128) + u, 1), :] = x[:, u * 128 : (u + 1) * 128]
         return carry
 
     lax.fori_loop(0, npair // rows, dense, 0)
@@ -158,8 +166,8 @@
     nodes = table.shape[0]
     return pl.pallas_call(
         functools.partial(score_kernel, npair=npair),
-        out_shape=jax.ShapeDtypeStruct((npair // 512, 512), jnp.float32),
-        in_specs=[SMEM] * 3 + [ANY] * 2 + [VMEM] * 2,
+        out_shape=jax.ShapeDtypeStruct((npair // 128, 128), jnp.float32),
+        in_specs=[SMEM] + [ANY] * 4 + [VMEM] * 2,
         out_specs=VMEM,
         scratch_shapes=[
             pltpu.VMEM((nodes, 2, 128), jnp.bfloat16),
@@ -168,6 +176,9 @@
             pltpu.VMEM((4 * npair, 128), jnp.float32),
             pltpu.SemaphoreType.DMA,
             pltpu.SemaphoreType.DMA((2, WORDS)),
+            pltpu.SemaphoreType.DMA((2,)),
+            pltpu.SMEM((2 * npair,), jnp.int32),
+            pltpu.SMEM((2 * npair,), jnp.int32),
         ]
         + [pltpu.SMEM((2 * ids.shape[0] // (QUARTERS * WORDS),), jnp.int32)] * WORDS,
         compiler_params=pltpu.CompilerParams(vmem_limit_bytes=56 * 2**20),
@@ -194,10 +205,17 @@
     code = ends // share * FAN + look_up(ends, info[:, WORDS].reshape(-1)) - 1
     keys = ((code - 32) << 26) | ((ends & (share - 1)) << 13) | jnp.arange(2 * npair, dtype=jnp.int32)
     keys = lax.sort(keys)
+    node = keys >> 13
+    new = jnp.concatenate([jnp.ones((1,), jnp.int32), (node[1:] != node[:-1]).astype(jnp.int32)])
+    rank = jnp.cumsum(new) - 1
+    place = lax.sort(((keys & 8191) << 13) | rank) & 8191
+    moves = ends | (place << 17)
+    code = (keys >> 26) + 32
     marks = jnp.arange(QUARTERS * FAN + 1, dtype=jnp.int32)
-    starts = jnp.sum((code[None, :] < marks[:, None]).astype(jnp.int32), axis=1)
-    moves = ends | ((keys & 8191) << 17)
-    spots = ((keys >> 13) & (share - 1)) + (((keys >> 26) + 32) // FAN & 1) * share
+    starts = jnp.sum((code[None, :] < marks[:, None]).astype(jnp.int32) * new[None, :], axis=1)
+    spots = (node & (share - 1)) + (code // FAN & 1) * share
+    order = jnp.arange(2 * npair, dtype=jnp.int32) << 14
+    spots = lax.sort(spots | order | ((1 - new) << 28)) & 16383
     mats = jnp.concatenate([w_self, w_neigh, w_one, w_two], axis=0)
     vecs = jnp.stack([b_layer, b_one, b_two, w_out])
     loss = score(starts, spots, moves, ids, table, mats, vecs, npair)

time: 235 us -> 224 us (0.953)
  other arithmetic: 11.2 us -> 25.3 us
  Pallas kernels: 101 us -> 87.2 us
  waiting for transfers between devices: 48.7 us -> 38 us
    pallas_call x1, Pallas kernels: 81.5 us -> 68 us  [score(): pl.pallas_call(functools.partial(score_kernel, npair=npair), out_shape=ja...]
    sort x0 -> x2, other arithmetic: none -> 13.5 us  [the longest x1 6.76 us: on_device(): place = lax.sort((keys & 8191) << 13 | rank) & 8191]
    all_gather x1, waiting for transfers between devices: 48.7 us -> 38 us  [on_device(): table = lax.all_gather(slab, ('node', 'pair'), axis=0, tiled=True)]
    unnamed x24 -> x23, local copies, waits for them, and re-layouts: 5.36 us -> 4.01 us
  transfers between devices with their start and end apart: 1 -> 1, of which waited for: 1 -> 1; matrix products, arithmetic and copies ran while one was open for 7% -> 13% of each run, Pallas kernels for 8% -> 9%
where the time goes in v1:
time: 224 us
  Pallas kernels  87.2 us (39%)
  blocking collectives  53.6 us (24%)
  waiting for transfers between devices  38 us (17%)
  other arithmetic  25.3 us (11%)
  between operations  13.6 us (6%)
  local copies, waits for them, and re-layouts  6.16 us (3%)
    pallas_call x1, Pallas kernels, score(): pl.pallas_call(functools.partial(score_kernel, npair=npair), out_shape=ja...  68 us
    all_gather x1, blocking collectives, on_device(): info = lax.all_gather(info, 'node', axis=0)  43.2 us
    all_gather x1, waiting for transfers between devices, on_device(): table = lax.all_gather(slab, ('node', 'pair'), axis=0, tiled=True)  38 us
    pallas_call x1, Pallas kernels, look_up(): pl.pallas_call(functools.partial(look_up_kernel, step=STEP), out_shape=ja...  19.2 us
    all_to_all x1, blocking collectives, on_device(): lax.all_to_all(features.reshape(parts, span // parts, cols), 'pair', spli...  10.5 us
    sort x1, other arithmetic, on_device(): place = lax.sort((keys & 8191) << 13 | rank) & 8191  6.76 us
    sort x1, other arithmetic, on_device(): spots = lax.sort(spots | order | 1 - new << 28) & 16383  6.76 us
    sort x1, other arithmetic, on_device(): keys = lax.sort(keys)  6.76 us
  transfers between devices with their start and end apart: 1, of which 1 were waited for; matrix products, arithmetic and copies ran while one was open for 13% of the time, Pallas kernels for 9%

profile of v1, /device:TPU:1, one launch (start us, length us, event | category | flops | bytes accessed | tf_op | source)
XLA Modules:
  0.0 223.9 jit_solution(10403538174833600380)
XLA Ops:
  6.5 0.8 copy-done
  7.4 10.5 %all_to_all.5 = bf16[8,128,32]{1,2,0:T(8,128)(2,1)S(1)} all-to-all(bf16[8,128,32]{1,2,0:T(8,128)(2,1)S(1)} %copy_bitcast_fusion), channel_id=1, replica_groups=mesh['pair'=8,'node'=32] {'pair'}, dimensions={0} | all-to-all | bytes 131072 | tf_op jit(solution)/shard_map/all_to_all | solution.py:194
  17.9 0.7 copy.24
  18.6 0.8 copy.31
  19.5 1.4 copy.27
  20.8 0.7 add_bitcast_fusion
  21.5 43.2 %all-gather.1 = s32[32,6,1024]{2,1,0:T(8,128)S(1)} all-gather(s32[1,6,1024]{2,1,0:T(8,128)S(1)} %add_bitcast_fusion), channel_id=2, replica_groups=mesh['pair'=8,'node'=32] {'node'}, dimensions={0}, use_global_device_ids=true | all-gather | bytes 811008 | tf_op jit(solution)/shard_map/all_gather | solution.py:201
  64.7 0.8 slice.33
  65.5 19.2 %shard_map.118 = s32[8192]{0:T(1024)} custom-call(s32[8192]{0:T(1024)} %bitcast.36, s32[32768]{0:T(1024)} %bitcast.39), custom_call_target="tpu_custom_call" | custom-call | bytes 33554432 | tf_op jit(solution)/shard_map/pallas_call | solution.py:31
  84.7 0.8 fusion.6
  85.5 6.8 %sort.42 = (s32[8192]{0:T(1024)S(1)}, s32[8192]{0:T(1024)}) sort(s32[8192]{0:T(1024)S(1)} %fusion.6, s32[8192]{0:T(1024)S(1)} %iota.20), dimensions={0}, to_apply=%region_0.1 | sort | flops 106496 | bytes 131072 | tf_op jit(solution)/shard_map/sort | solution.py:207
  92.5 0.3 reduce-window.9
  92.8 0.1 reduce-window.12
  93.0 0.4 copy.22
  93.4 1.0 copy.28
  94.4 0.1 slice_reduce_fusion
  94.6 6.8 %sort.44 = (s32[8192]{0:T(1024)S(1)}, s32[8192]{0:T(1024)}) sort(s32[8192]{0:T(1024)S(1)} %get-tuple-element.14, s32[8192]{0:T(1024)S(1)} %iota.23), dimensions={0}, to_apply=%region_5.6 | sort | flops 106496 | bytes 131072 | tf_op jit(solution)/shard_map/sort | solution.py:211
  101.4 6.8 %sort.43 = (s32[8192]{0:T(1024)S(1)}, s32[8192]{0:T(1024)}) sort(s32[8192]{0:T(1024)S(1)} %get-tuple-element.15, s32[8192]{0:T(1024)S(1)} %iota.22), dimensions={0}, to_apply=%region_2.3 | sort | flops 106496 | bytes 131072 | tf_op jit(solution)/shard_map/sort | solution.py:218
  108.1 0.6 pad_maximum_fusion.1.refs_6_
  108.7 0.8 pad_maximum_fusion.refs_5_
  109.6 0.8 select_reduce_fusion.refs_0_
  110.4 0.6 shift-left_or_fusion
  111.0 38.0 %all-gather.4.cloned.1.call-done.refs_4_ = bf16[32768,2,128]{2,1,0:T(2,128)(2,1)} async-done(((bf16[128,2,128]{2,1,0:T(2,128)(2,1)}), bf16[32768,2,128]{2,1,0:T(2,128)(2,1)}) %all-gather.4.cloned.1.call-update) | async-done | bytes 16777232 | tf_op jit(solution)/shard_map/all_gather | solution.py:198
  149.0 68.0 %shard_map.119 = f32[32,128]{1,0:T(8,128)} custom-call(s32[41]{0:T(128)} %select_reduce_fusion.refs_0_, s32[8192]{0:T(1024)} %get-tuple-element.20.refs_1_, s32[8192]{0:T(1024)} %get-tuple-element.19.refs_2_, s32[163840]{0:T(1024)} %bitcast.34, bf16[32768,2,128]{2,1,0:T(2,128)(2,1)} %all-gather.4.cloned.1.call-done.refs_4_, ...), custom_call_target="tpu_custom_call" | custom-call | tf_op jit(solution)/shard_map/pallas_call | solution.py:167
  (33 shorter events, 0.5 us)
Async XLA Ops:
  6.5 0.8 copy-start
  6.5 142.5 %all-gather.4.cloned.1.call-start = ((), (), s32[]{:S(2)}) async-start(), calls=%async_computation.1 | async-start | bytes 16842752 | tf_op jit(solution)/shard_map/all_gather | solution.py:198
  20.8 63.9 %copy-start.1 = (s32[1,32,2,128]{3,1,2,0:T(8,128)S(1)}, s32[1,32,2,128]{3,1,2,0:T(8,128)}, u32[]{:S(2)}) copy-start(s32[1,32,2,128]{3,1,2,0:T(8,128)} %copy.27) | copy-start | bytes 98308
  92.9 15.2 %copy-start.6 = (f32[256]{0:T(256)S(1)}, f32[256]{0:T(256)}, u32[]{:S(2)}) copy-start(f32[256]{0:T(256)} %param.23) | copy-start | bytes 3076
  92.9 15.2 %copy-start.7 = (f32[256]{0:T(256)S(1)}, f32[256]{0:T(256)}, u32[]{:S(2)}) copy-start(f32[256]{0:T(256)} %param.22) | copy-start | bytes 3076
  92.9 15.2 %copy-start.8 = (f32[256]{0:T(256)S(1)}, f32[256]{0:T(256)}, u32[]{:S(2)}) copy-start(f32[256]{0:T(256)} %param.20) | copy-start | bytes 3076
  93.0 15.2 %copy-start.9 = (f32[256]{0:T(256)S(1)}, f32[256]{0:T(256)}, u32[]{:S(2)}) copy-start(f32[256]{0:T(256)} %param.18) | copy-start | bytes 3076
  93.0 15.8 %copy-start.2 = (bf16[256,256]{1,0:T(8,128)(2,1)S(1)}, bf16[256,256]{1,0:T(8,128)(2,1)}, u32[]{:S(2)}) copy-start(bf16[256,256]{1,0:T(8,128)(2,1)} %param.21) | copy-start | bytes 393220
  93.0 15.8 %copy-start.3 = (bf16[256,256]{1,0:T(8,128)(2,1)S(1)}, bf16[256,256]{1,0:T(8,128)(2,1)}, u32[]{:S(2)}) copy-start(bf16[256,256]{1,0:T(8,128)(2,1)} %param.19) | copy-start | bytes 393220
  93.0 15.7 %copy-start.4 = (bf16[256,256]{1,0:T(8,128)(2,1)S(1)}, bf16[256,256]{1,0:T(8,128)(2,1)}, u32[]{:S(2)}) copy-start(bf16[256,256]{1,0:T(8,128)(2,1)} %param.17) | copy-start | bytes 393220
  93.0 15.7 %copy-start.5 = (bf16[256,256]{1,0:T(8,128)(2,1)S(1)}, bf16[256,256]{1,0:T(8,128)(2,1)}, u32[]{:S(2)}) copy-start(bf16[256,256]{1,0:T(8,128)(2,1)} %param.16) | copy-start | bytes 393220
Sparse Core Ops, SparseCore 0:
  18.7 130.2 all-gather.3

commit v2 on v1

--- a/solution.py
+++ b/solution.py
@@ -10,9 +10,9 @@
 FAN = 10
 WORDS = FAN // 2
 STEP = 16
-MOVES = 32
+MOVES = 128
 ROWS = 1024
-STEPS = (12, 12, 12, 12, 12, 12, 12, 12, 12, 12)
+STEPS = (16, 16, 16, 16, 16, 16, 16, 16, 16, 16)
 SMEM = pl.BlockSpec(memory_space=pltpu.SMEM)
 VMEM = pl.BlockSpec(memory_space=pltpu.VMEM)
 ANY = pl.BlockSpec(memory_space=pl.ANY)
@@ -101,12 +101,9 @@
                     means[pl.ds(2 * i + 2 * u, 2), :] = got[u]
                 return i + step
 
-            def rest(i, c=c):
-                means[pl.ds(2 * i, 2), :] = one(i, c)
-                return i + 1
-
             lo = lax.while_loop(lambda i: i <= hi - step, body, lo)
-            lax.while_loop(lambda i: i < hi, rest, lo)
+            lo = lax.while_loop(lambda i: i <= hi - 3, functools.partial(body, step=3), lo)
+            lax.while_loop(lambda i: i < hi, functools.partial(body, step=1), lo)
         return carry
 
     lax.fori_loop(0, QUARTERS, quarter, 0)

time: 224 us -> 221 us (0.987)
  Pallas kernels: 87.2 us -> 84.3 us
    pallas_call x1, Pallas kernels: 68 us -> 65.1 us  [score(): pl.pallas_call(functools.partial(score_kernel, npair=npair), out_shape=ja...]
where the time goes in v2:
time: 221 us
  Pallas kernels  84.3 us (38%)
  blocking collectives  53.6 us (24%)
  waiting for transfers between devices  38 us (17%)
  other arithmetic  25.3 us (11%)
  between operations  13.6 us (6%)
  local copies, waits for them, and re-layouts  6.16 us (3%)
    pallas_call x1, Pallas kernels, score(): pl.pallas_call(functools.partial(score_kernel, npair=npair), out_shape=ja...  65.1 us
    all_gather x1, blocking collectives, on_device(): info = lax.all_gather(info, 'node', axis=0)  43.2 us
    all_gather x1, waiting for transfers between devices, on_device(): table = lax.all_gather(slab, ('node', 'pair'), axis=0, tiled=True)  38 us
    pallas_call x1, Pallas kernels, look_up(): pl.pallas_call(functools.partial(look_up_kernel, step=STEP), out_shape=ja...  19.2 us
    all_to_all x1, blocking collectives, on_device(): lax.all_to_all(features.reshape(parts, span // parts, cols), 'pair', spli...  10.5 us
    sort x1, other arithmetic, on_device(): place = lax.sort((keys & 8191) << 13 | rank) & 8191  6.76 us
    sort x1, other arithmetic, on_device(): spots = lax.sort(spots | order | 1 - new << 28) & 16383  6.76 us
    sort x1, other arithmetic, on_device(): keys = lax.sort(keys)  6.76 us
  transfers between devices with their start and end apart: 1, of which 1 were waited for; matrix products, arithmetic and copies ran while one was open for 13% of the time, Pallas kernels for 9%

profile of v2, /device:TPU:1, one launch (start us, length us, event | category | flops | bytes accessed | tf_op | source)
XLA Modules:
  0.0 220.9 jit_solution(6661971616860096705)
XLA Ops:
  6.5 0.8 copy-done
  7.4 10.5 %all_to_all.5 = bf16[8,128,32]{1,2,0:T(8,128)(2,1)S(1)} all-to-all(bf16[8,128,32]{1,2,0:T(8,128)(2,1)S(1)} %copy_bitcast_fusion), channel_id=1, replica_groups=mesh['pair'=8,'node'=32] {'pair'}, dimensions={0} | all-to-all | bytes 131072 | tf_op jit(solution)/shard_map/all_to_all | solution.py:191
  17.9 0.7 copy.24
  18.6 0.8 copy.31
  19.5 1.4 copy.27
  20.8 0.7 add_bitcast_fusion
  21.5 43.2 %all-gather.1 = s32[32,6,1024]{2,1,0:T(8,128)S(1)} all-gather(s32[1,6,1024]{2,1,0:T(8,128)S(1)} %add_bitcast_fusion), channel_id=2, replica_groups=mesh['pair'=8,'node'=32] {'node'}, dimensions={0}, use_global_device_ids=true | all-gather | bytes 811008 | tf_op jit(solution)/shard_map/all_gather | solution.py:198
  64.7 0.8 slice.33
  65.5 19.2 %shard_map.118 = s32[8192]{0:T(1024)} custom-call(s32[8192]{0:T(1024)} %bitcast.36, s32[32768]{0:T(1024)} %bitcast.39), custom_call_target="tpu_custom_call" | custom-call | bytes 33554432 | tf_op jit(solution)/shard_map/pallas_call | solution.py:31
  84.7 0.8 fusion.6
  85.5 6.8 %sort.42 = (s32[8192]{0:T(1024)S(1)}, s32[8192]{0:T(1024)}) sort(s32[8192]{0:T(1024)S(1)} %fusion.6, s32[8192]{0:T(1024)S(1)} %iota.20), dimensions={0}, to_apply=%region_0.1 | sort | flops 106496 | bytes 131072 | tf_op jit(solution)/shard_map/sort | solution.py:204
  92.5 0.3 reduce-window.9
  92.8 0.1 reduce-window.12
  93.0 0.4 copy.22
  93.4 1.0 copy.28
  94.4 0.1 slice_reduce_fusion
  94.6 6.8 %sort.44 = (s32[8192]{0:T(1024)S(1)}, s32[8192]{0:T(1024)}) sort(s32[8192]{0:T(1024)S(1)} %get-tuple-element.14, s32[8192]{0:T(1024)S(1)} %iota.23), dimensions={0}, to_apply=%region_5.6 | sort | flops 106496 | bytes 131072 | tf_op jit(solution)/shard_map/sort | solution.py:208
  101.4 6.8 %sort.43 = (s32[8192]{0:T(1024)S(1)}, s32[8192]{0:T(1024)}) sort(s32[8192]{0:T(1024)S(1)} %get-tuple-element.15, s32[8192]{0:T(1024)S(1)} %iota.22), dimensions={0}, to_apply=%region_2.3 | sort | flops 106496 | bytes 131072 | tf_op jit(solution)/shard_map/sort | solution.py:215
  108.1 0.6 pad_maximum_fusion.1.refs_6_
  108.7 0.8 pad_maximum_fusion.refs_5_
  109.6 0.8 select_reduce_fusion.refs_0_
  110.4 0.6 shift-left_or_fusion
  111.0 38.0 %all-gather.4.cloned.1.call-done.refs_4_ = bf16[32768,2,128]{2,1,0:T(2,128)(2,1)} async-done(((bf16[128,2,128]{2,1,0:T(2,128)(2,1)}), bf16[32768,2,128]{2,1,0:T(2,128)(2,1)}) %all-gather.4.cloned.1.call-update) | async-done | bytes 16777232 | tf_op jit(solution)/shard_map/all_gather | solution.py:195
  149.0 65.1 %shard_map.119 = f32[32,128]{1,0:T(8,128)} custom-call(s32[41]{0:T(128)} %select_reduce_fusion.refs_0_, s32[8192]{0:T(1024)} %get-tuple-element.20.refs_1_, s32[8192]{0:T(1024)} %get-tuple-element.19.refs_2_, s32[163840]{0:T(1024)} %bitcast.34, bf16[32768,2,128]{2,1,0:T(2,128)(2,1)} %all-gather.4.cloned.1.call-done.refs_4_, ...), custom_call_target="tpu_custom_call" | custom-call | tf_op jit(solution)/shard_map/pallas_call | solution.py:164
  (33 shorter events, 0.5 us)
Async XLA Ops:
  6.5 0.8 copy-start
  6.5 142.5 %all-gather.4.cloned.1.call-start = ((), (), s32[]{:S(2)}) async-start(), calls=%async_computation.1 | async-start | bytes 16842752 | tf_op jit(solution)/shard_map/all_gather | solution.py:195
  20.8 63.9 %copy-start.1 = (s32[1,32,2,128]{3,1,2,0:T(8,128)S(1)}, s32[1,32,2,128]{3,1,2,0:T(8,128)}, u32[]{:S(2)}) copy-start(s32[1,32,2,128]{3,1,2,0:T(8,128)} %copy.27) | copy-start | bytes 98308
  92.9 15.2 %copy-start.6 = (f32[256]{0:T(256)S(1)}, f32[256]{0:T(256)}, u32[]{:S(2)}) copy-start(f32[256]{0:T(256)} %param.23) | copy-start | bytes 3076
  92.9 15.2 %copy-start.7 = (f32[256]{0:T(256)S(1)}, f32[256]{0:T(256)}, u32[]{:S(2)}) copy-start(f32[256]{0:T(256)} %param.22) | copy-start | bytes 3076
  92.9 15.2 %copy-start.8 = (f32[256]{0:T(256)S(1)}, f32[256]{0:T(256)}, u32[]{:S(2)}) copy-start(f32[256]{0:T(256)} %param.20) | copy-start | bytes 3076
  93.0 15.2 %copy-start.9 = (f32[256]{0:T(256)S(1)}, f32[256]{0:T(256)}, u32[]{:S(2)}) copy-start(f32[256]{0:T(256)} %param.18) | copy-start | bytes 3076
  93.0 15.8 %copy-start.2 = (bf16[256,256]{1,0:T(8,128)(2,1)S(1)}, bf16[256,256]{1,0:T(8,128)(2,1)}, u32[]{:S(2)}) copy-start(bf16[256,256]{1,0:T(8,128)(2,1)} %param.21) | copy-start | bytes 393220
  93.0 15.8 %copy-start.3 = (bf16[256,256]{1,0:T(8,128)(2,1)S(1)}, bf16[256,256]{1,0:T(8,128)(2,1)}, u32[]{:S(2)}) copy-start(bf16[256,256]{1,0:T(8,128)(2,1)} %param.19) | copy-start | bytes 393220
  93.0 15.7 %copy-start.4 = (bf16[256,256]{1,0:T(8,128)(2,1)S(1)}, bf16[256,256]{1,0:T(8,128)(2,1)}, u32[]{:S(2)}) copy-start(bf16[256,256]{1,0:T(8,128)(2,1)} %param.17) | copy-start | bytes 393220
  93.0 15.7 %copy-start.5 = (bf16[256,256]{1,0:T(8,128)(2,1)S(1)}, bf16[256,256]{1,0:T(8,128)(2,1)}, u32[]{:S(2)}) copy-start(bf16[256,256]{1,0:T(8,128)(2,1)} %param.16) | copy-start | bytes 393220
Sparse Core Ops, SparseCore 0:
  18.7 130.2 all-gather.3
